TPU v7x, 32 devices: a whole 2x2x4 slice. The times are simulated.
32 devices in a mesh: table: 2 (over x), image: 16 (over z, y, core).
Axes of the slice: x: 2, y: 2, z: 4, core: 2. Of those that a mesh axis runs over, the one named last changes fastest.
Arguments:
- traces: bfloat16 [512, 1920], P(('table', 'image')), may hold values from -6 to 6
- aperture: int32 [512, 4], P(('table', 'image')), may hold values from 0 to 15, all different within a row; in each aligned block of 16 rows (0 to 15, 16 to 31, ...) at most 8 rows name the same one
- bucket: int32 [512], P(('table', 'image')), may hold values from 0 to 3
- table_node: int32 [512, 4], P(('table', 'image')), may hold values from 0 to 15
- entry_gain: bfloat16 [512, 4], P(('table', 'image')), may hold values from 0.5 to 2
- travel: float32 [16, 16, 1024], P('image', None, 'table'), may hold values from 1 to 1918
- spread: float32 [16, 16, 1024], P('image', None, 'table'), may hold values from 0.1 to 1
Outputs:
- image: float32 [16, 1024], P('image', 'table')
Inputs may be any that keep to these rules, and one draw needn't show every extreme that they name: `aperture`: each trace names 4 different tiles. Among the 16 traces of one device at most 8 name the same tile, and in every draw some tile is named by exactly 8 of them.
All inputs are finite; a program needn't handle non-finite values.
Results may differ from a plain program's by a relative error of at most 0.0024.
Values may be sent and summed in bfloat16 or wider, within the bound.
A program may use at most 128 MiB of HBM per device.

v0:
```python
import math
import jax
import jax.numpy as jnp
from jax import lax
from jax.sharding import PartitionSpec as P

max_lag = 7


def antialias(trace_rows, filter_index):
    half_width = (2 + 2 * filter_index).astype(jnp.float32)[..., None]
    length = trace_rows.shape[-1]
    widths = [(0, 0)] * (trace_rows.ndim - 1) + [(max_lag, max_lag)]
    padded = jnp.pad(trace_rows, widths)
    summed = jnp.zeros(trace_rows.shape, jnp.float32)
    for sample_lag in range(-max_lag, max_lag + 1):
        ramp_weight = jnp.maximum(half_width - abs(sample_lag), 0.0) / (half_width * half_width)
        window = lax.slice_in_dim(
            padded, max_lag + sample_lag, max_lag + sample_lag + length, axis=trace_rows.ndim - 1
        )
        summed = summed + ramp_weight * window
    return summed


def interpolate(stack_tile, travel_tile, spread_tile):
    floor_value = jnp.floor(travel_tile)
    fraction = travel_tile - floor_value
    lower_index = floor_value.astype(jnp.int32)
    shifted = jnp.pad(stack_tile[:, 1:], ((0, 0), (0, 1)))
    paired = jnp.stack([stack_tile, shifted], axis=-1)
    picked = jnp.take_along_axis(paired, lower_index[:, :, None], axis=1)
    lower_value = picked[:, :, 0]
    upper_value = picked[:, :, 1]
    return jnp.sum(spread_tile * ((1.0 - fraction) * lower_value + fraction * upper_value), axis=0)


def per_device(traces, aperture, bucket, table_node, entry_gain, travel, spread):
    tiles = lax.axis_size("image")
    groups = lax.axis_size("table")
    trace_count, samples = traces.shape
    aper_count = aperture.shape[1]
    node_count = travel.shape[1]
    capacity = max(2, 2 * trace_count * aper_count // tiles)
    entries = trace_count * aper_count
    destination = aperture.reshape(entries)
    member = (destination[:, None] == jnp.arange(tiles, dtype=jnp.int32)[None, :]).astype(jnp.int32)
    earlier = jnp.cumsum(member, axis=0) - member
    slot_index = jnp.sum(earlier * member, axis=1)
    source_row = jnp.arange(entries, dtype=jnp.int32) // aper_count
    flat_nodes = table_node.reshape(entries)
    flat_gains = entry_gain.reshape(entries)
    node_slots = jnp.zeros((capacity, tiles), jnp.int32).at[slot_index, destination].set(flat_nodes)
    raw_slots = (
        jnp.zeros((capacity, tiles, samples), jnp.bfloat16)
        .at[slot_index, destination]
        .set(traces[source_row])
    )
    gain_slots = (
        jnp.zeros((capacity, tiles), jnp.bfloat16).at[slot_index, destination].set(flat_gains)
    )
    filter_slots = (
        jnp.zeros((capacity, tiles), jnp.int32).at[slot_index, destination].set(bucket[source_row])
    )
    raw_part = lax.all_to_all(raw_slots, "image", split_axis=1, concat_axis=1, tiled=True)
    gain_part = lax.all_to_all(gain_slots, "image", split_axis=1, concat_axis=1, tiled=True)
    filter_part = lax.all_to_all(filter_slots, "image", split_axis=1, concat_axis=1, tiled=True)
    node_part = lax.all_to_all(node_slots, "image", split_axis=1, concat_axis=1, tiled=True)
    filtered = antialias(raw_part.astype(jnp.float32), filter_part)
    weighted = (gain_part.astype(jnp.float32)[..., None] * filtered).astype(jnp.bfloat16)
    slot_total = tiles * capacity
    flat_values = weighted.reshape(slot_total, samples)
    node_member = (
        node_part.reshape(slot_total)[:, None] == jnp.arange(node_count, dtype=jnp.int32)[None, :]
    ).astype(jnp.bfloat16)
    stack = lax.dot_general(
        node_member, flat_values, (((0,), (0,)), ((), ())), preferred_element_type=jnp.float32
    )
    scale = 1.0 / math.sqrt(trace_count * groups * aper_count)
    summed_stack = lax.psum(stack, "table")
    return (interpolate(summed_stack, travel[0], spread[0]) * scale)[None, :]


def solution(mesh):
    in_specs = (
        P(("table", "image"), None),
        P(("table", "image"), None),
        P(("table", "image")),
        P(("table", "image"), None),
        P(("table", "image"), None),
        P("image", None, "table"),
        P("image", None, "table"),
    )
    out_specs = P("image", "table")
    return jax.shard_map(
        per_device, mesh=mesh, in_specs=in_specs, out_specs=out_specs, check_vma=False
    )
```

profile of v0, /device:TPU:0, one launch (start us, length us, event | category | flops | bytes accessed | tf_op | source)
XLA Modules:
  0.0 235.3 jit_solution(4942274203572084065)
XLA Ops:
  6.5 0.0 copy-start
  6.5 0.8 copy.41
  7.3 0.1 eq.30
  7.4 0.1 reshape.171
  7.5 0.1 fusion.22
  7.6 0.1 reduce_window_sum.11
  7.7 0.2 select_reduce_fusion
  7.8 0.8 copy.46
  8.6 0.1 reshape.206
  8.7 3.5 %scatter_fusion.1 = bf16[8,16]{1,0:T(8,128)(2,1)S(1)} fusion(bf16[8,16]{1,0:T(8,128)(2,1)S(1)} %broadcast_in_dim.11, s32[64]{0:T(128)S(1)} %fusion.25, bf16[64]{0:T(256)(128)(2,1)S(1)} %reshape.206), kind=kCustom, calls=%fused_computation.4 | custom fusion | bytes 896 | tf_op jit(solution)/shard_map/scatter | solution.py:59
  12.3 0.7 copy.47
  12.9 7.4 %all-to-all-start.1 = ((bf16[8,16,1]{0,2,1:T(2,128)(2,1)}), bf16[8,16,1]{0,2,1:T(2,128)(2,1)S(1)}, u32[]{:S(2)}, u32[]{:S(2)}) async-start(bf16[8,16,1]{0,2,1:T(2,128)(2,1)} %copy.47), calls=%async_computation.1 | async-start | bytes 16384 | tf_op jit(solution)/shard_map/all_to_all | solution.py:65
  20.4 1.4 gather_fusion
  21.8 3.5 %scatter_fusion.2 = s32[8,16]{1,0:T(8,128)S(1)} fusion(s32[8,16]{1,0:T(8,128)S(1)} %broadcast.222.clone, s32[64]{0:T(128)S(1)} %fusion.25, s32[64]{0:T(128)S(1)} %gather_fusion), kind=kCustom, calls=%fused_computation.5 | custom fusion | bytes 1280 | tf_op jit(solution)/shard_map/scatter | solution.py:62
  25.3 0.7 copy.49
  25.9 0.8 all-to-all-done.1
  26.7 5.2 %all-to-all-start.2 = ((s32[8,16,1]{0,2,1:T(1,128)}), s32[8,16,1]{0,2,1:T(1,128)S(1)}, u32[]{:S(2)}, u32[]{:S(2)}) async-start(s32[8,16,1]{0,2,1:T(1,128)} %copy.49), calls=%async_computation.2 | async-start | bytes 16384 | tf_op jit(solution)/shard_map/all_to_all | solution.py:66
  31.9 0.8 copy.43
  32.7 0.1 reshape.200
  32.8 3.5 %scatter_fusion = s32[8,16]{1,0:T(8,128)S(1)} fusion(s32[8,16]{1,0:T(8,128)S(1)} %broadcast.222.clone.1, s32[64]{0:T(128)S(1)} %fusion.25, s32[64]{0:T(128)S(1)} %reshape.200), kind=kCustom, calls=%fused_computation.3 | custom fusion | bytes 1280 | tf_op jit(solution)/shard_map/scatter | solution.py:52
  36.3 0.7 copy.44
  36.9 1.4 all-to-all-done.2
  38.4 4.6 %all-to-all-start = ((s32[8,16,1]{0,2,1:T(1,128)}), s32[8,16,1]{0,2,1:T(1,128)S(1)}, u32[]{:S(2)}, u32[]{:S(2)}) async-start(s32[8,16,1]{0,2,1:T(1,128)} %copy.44), calls=%async_computation | async-start | bytes 16384 | tf_op jit(solution)/shard_map/all_to_all | solution.py:67
  43.0 0.0 copy-done
  43.0 0.0 copy-start.1
  43.0 0.8 gather_fusion.1
  43.8 6.3 %scatter_fusion.3 = bf16[8,16,1920]{2,1,0:T(8,128)(2,1)S(1)} fusion(bf16[8,16,1920]{2,1,0:T(8,128)(2,1)S(1)} %broadcast_in_dim.12, s32[64]{0:T(128)S(1)} %fusion.25, bf16[64,1920]{1,0:T(8,128)(2,1)S(1)} %gather_fusion.1), kind=kCustom, calls=%fused_computation.6 | custom fusion | bytes 737792 | tf_op jit(solution)/shard_map/scatter | solution.py:56
  50.1 0.9 copy.51
  50.9 0.0 all-to-all-done
  50.9 6.0 %all-to-all-start.3 = ((bf16[8,16,1920]{2,0,1:T(8,128)(2,1)}), bf16[8,16,1920]{2,0,1:T(8,128)(2,1)S(1)}, u32[]{:S(2)}, u32[]{:S(2)}) async-start(bf16[8,16,1920]{2,0,1:T(8,128)(2,1)} %copy.51), calls=%async_computation.3 | async-start | bytes 983040 | tf_op jit(solution)/shard_map/all_to_all | solution.py:64
  56.9 0.0 all-reduce.4.cloned.1.call-start
  57.0 0.0 copy-done.1
  57.1 0.1 copy.48
  57.1 0.1 copy.45
  57.2 0.1 eq.34
  57.3 0.1 copy.50
  57.4 13.3 %all-to-all-done.3 = bf16[8,16,1920]{2,0,1:T(8,128)(2,1)S(1)} async-done(((bf16[8,16,1920]{2,0,1:T(8,128)(2,1)}), bf16[8,16,1920]{2,0,1:T(8,128)(2,1)S(1)}, u32[]{:S(2)}, u32[]{:S(2)}) %all-to-all-start.3) | async-done | bytes 491552 | tf_op jit(solution)/shard_map/all_to_all | solution.py:64
  70.7 0.1 copy_convert_fusion
  70.8 4.0 %multiply_convert_fusion = bf16[8,16,1920]{2,1,0:T(8,128)(2,1)S(1)} fusion(f32[8,16,1920]{2,1,0:T(8,128)S(1)} %copy_convert_fusion, f32[8,16]{1,0:T(8,128)S(1)} %get-tuple-element.6, f32[8,16]{1,0:T(8,128)S(1)} %get-tuple-element.7, f32[8,16]{1,0:T(8,128)S(1)} %get-tuple-element.8, f32[8,16]{1,0:T(8,128)S(1)} %get-tuple-element.9, ...), kind=kLoop, calls=%fused_computation.7 | loop fusion | flops 7618560 | bytes 1479168 | tf_op jit(solution)/shard_map/convert_element_type | solution.py:69
  74.8 0.9 fusion.11
  75.7 0.0 all-reduce.4.cloned.1.call-update
  75.8 20.8 %all-reduce.4.cloned.1.call-done = f32[16,1920]{1,0:T(8,128)} async-done(((f32[16,1920]{1,0:T(8,128)}), f32[16,1920]{1,0:T(8,128)}) %all-reduce.4.cloned.1.call-update) | async-done | bytes 122896 | tf_op jit(solution)/shard_map/psum | solution.py:79
  96.6 1.0 slice.83
  97.6 0.9 pad_maximum_fusion
  98.6 7.8 %copy.53 = f32[16,1920,2]{2,1,0:T(8,128)} copy(f32[16,1920,2]{1,0,2:T(8,128)S(1)} %pad_maximum_fusion) | data formatting | bytes 491520 | tf_op jit(solution)/shard_map/stack | solution.py:30
  106.3 118.6 %gather_fusion.2 = f32[8192,2]{1,0:T(8,128)} fusion(f32[16,1920,2]{2,1,0:T(8,128)} %copy.53, s32[8192]{0:T(1024)S(1)} %bitcast.70), kind=kCustom, calls=%fused_computation.2 | custom fusion | bytes 196608 | tf_op jit(solution)/shard_map/jit(take_along_axis)/gather | solution.py:31
  225.0 0.0 copy-start.2
  225.0 2.8 %copy.54 = f32[16,512,2]{1,0,2:T(8,128)S(1)} copy(f32[16,512,2]{2,1,0:T(8,128)} %bitcast.74) | data formatting | bytes 131072 | tf_op jit(solution)/shard_map/jit(take_along_axis)/gather | solution.py:31
  227.8 0.0 copy-done.2
  227.9 0.6 broadcast_multiply_fusion
  (15 shorter events, 0.2 us)
Async XLA Ops:
  6.5 36.4 %copy-start = (bf16[16,1920]{1,0:T(8,128)(2,1)S(1)}, bf16[16,1920]{1,0:T(8,128)(2,1)}, u32[]{:S(2)}) copy-start(bf16[16,1920]{1,0:T(8,128)(2,1)} %param.7) | copy-start | bytes 184324
  12.9 13.8 %all-to-all-start.1 = ((bf16[8,16,1]{0,2,1:T(2,128)(2,1)}), bf16[8,16,1]{0,2,1:T(2,128)(2,1)S(1)}, u32[]{:S(2)}, u32[]{:S(2)}) async-start(bf16[8,16,1]{0,2,1:T(2,128)(2,1)} %copy.47), calls=%async_computation.1 | async-start | bytes 16384 | tf_op jit(solution)/shard_map/all_to_all | solution.py:65
  26.7 11.6 %all-to-all-start.2 = ((s32[8,16,1]{0,2,1:T(1,128)}), s32[8,16,1]{0,2,1:T(1,128)S(1)}, u32[]{:S(2)}, u32[]{:S(2)}) async-start(s32[8,16,1]{0,2,1:T(1,128)} %copy.49), calls=%async_computation.2 | async-start | bytes 16384 | tf_op jit(solution)/shard_map/all_to_all | solution.py:66
  38.4 12.6 %all-to-all-start = ((s32[8,16,1]{0,2,1:T(1,128)}), s32[8,16,1]{0,2,1:T(1,128)S(1)}, u32[]{:S(2)}, u32[]{:S(2)}) async-start(s32[8,16,1]{0,2,1:T(1,128)} %copy.44), calls=%async_computation | async-start | bytes 16384 | tf_op jit(solution)/shard_map/all_to_all | solution.py:67
  43.0 14.0 %copy-start.1 = (f32[1,16,512]{2,1,0:T(8,128)S(1)}, f32[1,16,512]{2,1,0:T(8,128)}, u32[]{:S(2)}) copy-start(f32[1,16,512]{2,1,0:T(8,128)} %param.12) | copy-start | bytes 98308
  50.9 19.8 %all-to-all-start.3 = ((bf16[8,16,1920]{2,0,1:T(8,128)(2,1)}), bf16[8,16,1920]{2,0,1:T(8,128)(2,1)S(1)}, u32[]{:S(2)}, u32[]{:S(2)}) async-start(bf16[8,16,1920]{2,0,1:T(8,128)(2,1)} %copy.51), calls=%async_computation.3 | async-start | bytes 983040 | tf_op jit(solution)/shard_map/all_to_all | solution.py:64
  56.9 39.7 %all-reduce.4.cloned.1.call-start = ((), (), s32[]{:S(2)}) async-start(), calls=%async_computation.4 | async-start | bytes 245760 | tf_op jit(solution)/shard_map/psum | solution.py:79
  225.0 2.9 %copy-start.2 = (f32[1,16,512]{2,1,0:T(8,128)S(1)}, f32[1,16,512]{2,1,0:T(8,128)}, u32[]{:S(2)}) copy-start(f32[1,16,512]{2,1,0:T(8,128)} %param.13) | copy-start | bytes 98308
Sparse Core Ops, SparseCore 0:
  75.9 20.6 all-reduce.3
where the time goes:
time: 236 us; the launch traced here: 235 us
  local copies, waits for them, and re-layouts  155 us (66%)
  waiting for transfers between devices  36.4 us (15%)
  starting transfers between devices  23.2 us (10%)
  between operations  13.6 us (6%)
  other arithmetic  6.02 us (3%)
    gather x2, local copies, waits for them, and re-layouts, interpolate(): picked = jnp.take_along_axis(paired, lower_index[:, :, None], axis=1)  121 us
    psum x1, waiting for transfers between devices, per_device(): summed_stack = lax.psum(stack, 'table')  20.8 us
    all_to_all x1, waiting for transfers between devices, per_device(): lax.all_to_all(raw_slots, 'image', split_axis=1, concat_axis=1, tiled=True)  13.3 us
    another operation x2, local copies, waits for them, and re-layouts, interpolate(): paired = jnp.stack([stack_tile, shifted], axis=-1)  7.79 us
    all_to_all x1, starting transfers between devices, per_device(): lax.all_to_all(gain_slots, 'image', split_axis=1, concat_axis=1, tiled=True)  7.39 us
    scatter x2, local copies, waits for them, and re-layouts, per_device(): raw_slots = jnp.zeros((capacity, tiles, samples), jnp.bfloat16).at[slot_i...  7.14 us
    scatter x2, local copies, waits for them, and re-layouts, per_device(): jnp.zeros((capacity, tiles), jnp.int32).at[slot_index, destination]  6.91 us
    all_to_all x1, starting transfers between devices, per_device(): lax.all_to_all(raw_slots, 'image', split_axis=1, concat_axis=1, tiled=True)  6.01 us
  transfers between devices with their start and end apart: 5, of which 4 were waited for; matrix products, arithmetic and copies ran while one was open for 8% of the time, Pallas kernels for 0%

commit v1 on v0

--- a/solution.py
+++ b/solution.py
@@ -61,7 +61,12 @@
     filter_slots = (
         jnp.zeros((capacity, tiles), jnp.int32).at[slot_index, destination].set(bucket[source_row])
     )
-    raw_part = lax.all_to_all(raw_slots, "image", split_axis=1, concat_axis=1, tiled=True)
+    raw_part = jnp.concatenate(
+        lax.all_to_all(
+            jnp.stack(jnp.split(raw_slots, lax.axis_size("image"), axis=1)), "image", 0, 0
+        ),
+        axis=1,
+    )
     gain_part = lax.all_to_all(gain_slots, "image", split_axis=1, concat_axis=1, tiled=True)
     filter_part = lax.all_to_all(filter_slots, "image", split_axis=1, concat_axis=1, tiled=True)
     node_part = lax.all_to_all(node_slots, "image", split_axis=1, concat_axis=1, tiled=True)

time: 236 us -> 248 us (1.051)
  local copies, waits for them, and re-layouts: 155 us -> 164 us
  waiting for transfers between devices: 36.4 us -> 40.7 us
    unnamed x10 -> x29, local copies, waits for them, and re-layouts: 2.33 us -> 10.8 us
    all_to_all x1, waiting for transfers between devices: 0.01 us -> 5.79 us  [per_device(): lax.all_to_all(node_slots, 'image', split_axis=1, concat_axis=1, tiled=True)]
    scatter x2 -> x1, local copies, waits for them, and re-layouts: 7.14 us -> 6.29 us  [per_device(): raw_slots = jnp.zeros((capacity, tiles, samples), jnp.bfloat16).at[slot_i...]
  transfers between devices with their start and end apart: 5 -> 5, of which waited for: 4 -> 4; matrix products, arithmetic and copies ran while one was open for 8% -> 11% of each run, Pallas kernels for 0% -> 0%
where the time goes in v1:
time: 248 us; the launch traced here: 247 us
  local copies, waits for them, and re-layouts  164 us (66%)
  waiting for transfers between devices  40.7 us (16%)
  starting transfers between devices  21.5 us (9%)
  between operations  13.7 us (6%)
  other arithmetic  5.97 us (2%)
    gather x2, local copies, waits for them, and re-layouts, interpolate(): picked = jnp.take_along_axis(paired, lower_index[:, :, None], axis=1)  121 us
    psum x1, waiting for transfers between devices, per_device(): summed_stack = lax.psum(stack, 'table')  20.7 us
    all_to_all x1, waiting for transfers between devices, per_device(): lax.all_to_all(jnp.stack(jnp.split(raw_slots, lax.axis_size('image'), axi...  12.7 us
    unnamed x29, local copies, waits for them, and re-layouts  10.8 us
    another operation x2, local copies, waits for them, and re-layouts, interpolate(): paired = jnp.stack([stack_tile, shifted], axis=-1)  7.79 us
    all_to_all x1, starting transfers between devices, per_device(): lax.all_to_all(gain_slots, 'image', split_axis=1, concat_axis=1, tiled=True)  7.39 us
    scatter x2, local copies, waits for them, and re-layouts, per_device(): jnp.zeros((capacity, tiles), jnp.int32).at[slot_index, destination]  6.91 us
    scatter x1, local copies, waits for them, and re-layouts, per_device(): raw_slots = jnp.zeros((capacity, tiles, samples), jnp.bfloat16).at[slot_i...  6.29 us
  transfers between devices with their start and end apart: 5, of which 4 were waited for; matrix products, arithmetic and copies ran while one was open for 11% of the time, Pallas kernels for 0%

profile of v1, /device:TPU:0, one launch (start us, length us, event | category | flops | bytes accessed | tf_op | source)
XLA Modules:
  0.0 247.0 jit_solution(9768770589402737494)
XLA Ops:
  6.5 0.8 copy.389
  7.3 0.1 eq.30
  7.4 0.1 reshape.175
  7.5 0.1 fusion.22
  7.6 0.1 reduce_window_sum.11
  7.7 0.2 select_reduce_fusion
  7.8 0.8 copy.394
  8.6 0.1 reshape.211
  8.7 3.5 %scatter_fusion.1 = bf16[8,16]{1,0:T(8,128)(2,1)S(1)} fusion(bf16[8,16]{1,0:T(8,128)(2,1)S(1)} %broadcast_in_dim.11, s32[64]{0:T(128)S(1)} %fusion.25, bf16[64]{0:T(256)(128)(2,1)S(1)} %reshape.211), kind=kCustom, calls=%fused_computation.4 | custom fusion | bytes 896 | tf_op jit(solution)/shard_map/scatter | solution.py:59
  12.3 0.7 copy.395
  13.0 7.4 %all-to-all-start.1 = ((bf16[8,16,1]{0,2,1:T(2,128)(2,1)}), bf16[8,16,1]{0,2,1:T(2,128)(2,1)S(1)}, u32[]{:S(2)}, u32[]{:S(2)}) async-start(bf16[8,16,1]{0,2,1:T(2,128)(2,1)} %copy.395), calls=%async_computation.1 | async-start | bytes 16384 | tf_op jit(solution)/shard_map/all_to_all | solution.py:70
  20.4 0.8 gather_fusion.1
  21.2 6.3 %scatter_fusion.3 = bf16[8,16,1920]{2,1,0:T(8,128)(2,1)S(1)} fusion(bf16[8,16,1920]{2,1,0:T(8,128)(2,1)S(1)} %broadcast_in_dim.12, s32[64]{0:T(128)S(1)} %fusion.25, bf16[64,1920]{1,0:T(8,128)(2,1)S(1)} %gather_fusion.1), kind=kCustom, calls=%fused_computation.6 | custom fusion | bytes 737792 | tf_op jit(solution)/shard_map/scatter | solution.py:56
  27.5 0.8 fusion.26
  28.3 0.6 constant_dynamic-update-slice_fusion.15
  28.9 0.6 constant_dynamic-update-slice_fusion.14
  29.5 0.6 constant_dynamic-update-slice_fusion.13
  30.1 0.6 constant_dynamic-update-slice_fusion.12
  30.8 0.6 constant_dynamic-update-slice_fusion.11
  31.4 0.6 constant_dynamic-update-slice_fusion.10
  32.0 0.6 constant_dynamic-update-slice_fusion.9
  32.6 0.6 constant_dynamic-update-slice_fusion.8
  33.2 0.6 constant_dynamic-update-slice_fusion.7
  33.8 0.6 constant_dynamic-update-slice_fusion.6
  34.4 0.6 constant_dynamic-update-slice_fusion.5
  35.1 0.6 constant_dynamic-update-slice_fusion.4
  35.7 0.6 constant_dynamic-update-slice_fusion.3
  36.3 0.6 constant_dynamic-update-slice_fusion.2
  36.9 0.8 gather_fusion
  37.7 3.5 %scatter_fusion.2 = s32[8,16]{1,0:T(8,128)S(1)} fusion(s32[8,16]{1,0:T(8,128)S(1)} %broadcast.222.clone, s32[64]{0:T(128)S(1)} %fusion.25, s32[64]{0:T(128)S(1)} %gather_fusion), kind=kCustom, calls=%fused_computation.5 | custom fusion | bytes 1280 | tf_op jit(solution)/shard_map/scatter | solution.py:62
  41.1 0.7 copy.398
  41.8 6.0 %all-to-all-start.2 = ((s32[8,16,1]{0,2,1:T(1,128)}), s32[8,16,1]{0,2,1:T(1,128)S(1)}, u32[]{:S(2)}, u32[]{:S(2)}) async-start(s32[8,16,1]{0,2,1:T(1,128)} %copy.398), calls=%async_computation.2 | async-start | bytes 16384 | tf_op jit(solution)/shard_map/all_to_all | solution.py:71
  47.8 0.6 constant_dynamic-update-slice_fusion.1
  48.4 0.1 copy.391
  48.5 0.1 reshape.205
  48.6 3.5 %scatter_fusion = s32[8,16]{1,0:T(8,128)S(1)} fusion(s32[8,16]{1,0:T(8,128)S(1)} %broadcast.222.clone.1, s32[64]{0:T(128)S(1)} %fusion.25, s32[64]{0:T(128)S(1)} %reshape.205), kind=kCustom, calls=%fused_computation.3 | custom fusion | bytes 1280 | tf_op jit(solution)/shard_map/scatter | solution.py:52
  52.1 0.7 copy.392
  52.7 1.5 all-to-all-done.2
  54.2 4.5 %all-to-all-start = ((s32[8,16,1]{0,2,1:T(1,128)}), s32[8,16,1]{0,2,1:T(1,128)S(1)}, u32[]{:S(2)}, u32[]{:S(2)}) async-start(s32[8,16,1]{0,2,1:T(1,128)} %copy.392), calls=%async_computation | async-start | bytes 16384 | tf_op jit(solution)/shard_map/all_to_all | solution.py:72
  58.8 0.6 constant_dynamic-update-slice_fusion
  59.4 5.8 %all-to-all-done = s32[8,16,1]{0,2,1:T(1,128)S(1)} async-done(((s32[8,16,1]{0,2,1:T(1,128)}), s32[8,16,1]{0,2,1:T(1,128)S(1)}, u32[]{:S(2)}, u32[]{:S(2)}) %all-to-all-start) | async-done | bytes 544 | tf_op jit(solution)/shard_map/all_to_all | solution.py:72
  65.2 3.6 %all-to-all-start.3 = ((bf16[16,8,1,1920]{3,1,2,0:T(8,128)(2,1)}), bf16[16,8,1,1920]{3,1,2,0:T(8,128)(2,1)S(1)}, u32[]{:S(2)}, u32[]{:S(2)}) async-start(bf16[16,8,1,1920]{3,1,2,0:T(8,128)(2,1)} %constant_dynamic-update-slice_fusion), calls=%async_computation.3 | async-start | bytes 983040 | tf_op jit(solution)/shard_map/all_to_all | solution.py:65
  68.8 0.1 copy.396
  68.9 0.1 copy.397
  69.0 0.1 copy.399
  69.1 0.1 copy.400
  69.2 0.1 copy.401
  69.2 0.1 copy.402
  69.3 0.1 copy.403
  69.4 0.1 copy.404
  69.5 0.1 copy.405
  69.5 0.1 copy.406
  69.6 0.1 copy.407
  69.7 0.1 eq.34
  69.8 12.7 %all-to-all-done.3 = bf16[16,8,1,1920]{3,1,2,0:T(8,128)(2,1)S(1)} async-done(((bf16[16,8,1,1920]{3,1,2,0:T(8,128)(2,1)}), bf16[16,8,1,1920]{3,1,2,0:T(8,128)(2,1)S(1)}, u32[]{:S(2)}, u32[]{:S(2)}) %all-to-all-start.3) | async-done | bytes 491552 | tf_op jit(solution)/shard_map/all_to_all | solution.py:65
  82.5 3.9 %multiply_convert_fusion = bf16[8,16,1920]{2,0,1:T(8,128)(2,1)S(1)} fusion(f32[8,16,1920]{2,0,1:T(8,128)S(1)} %convert_bitcast_fusion, f32[8,16]{0,1:T(8,128)S(1)} %copy.407, f32[8,16]{0,1:T(8,128)S(1)} %copy.406, f32[8,16]{0,1:T(8,128)S(1)} %copy.405, f32[8,16]{0,1:T(8,128)S(1)} %copy.404, f32[8,16]{0,1:T(8,128)S(1)} %copy.403, f32[8,16]{0,1:T(8,128)S(1)} %copy.402, ...), kind=kLoop, calls=%fused_computation.8 | loop fusion | flops 7618560 | bytes 1479168 | tf_op jit(solution)/shard_map/convert_element_type | solution.py:74
  86.5 0.9 fusion.11
  87.5 20.7 %all-reduce.4.cloned.1.call-done = f32[16,1920]{1,0:T(8,128)} async-done(((f32[16,1920]{1,0:T(8,128)}), f32[16,1920]{1,0:T(8,128)}) %all-reduce.4.cloned.1.call-update) | async-done | bytes 122896 | tf_op jit(solution)/shard_map/psum | solution.py:84
  108.3 1.0 slice.83
  109.3 0.9 pad_maximum_fusion
  110.2 7.8 %copy.409 = f32[16,1920,2]{2,1,0:T(8,128)} copy(f32[16,1920,2]{1,0,2:T(8,128)S(1)} %pad_maximum_fusion) | data formatting | bytes 491520 | tf_op jit(solution)/shard_map/stack | solution.py:30
  118.0 118.6 %gather_fusion.2 = f32[8192,2]{1,0:T(8,128)} fusion(f32[16,1920,2]{2,1,0:T(8,128)} %copy.409, s32[8192]{0:T(1024)S(1)} %bitcast.106), kind=kCustom, calls=%fused_computation.2 | custom fusion | bytes 196608 | tf_op jit(solution)/shard_map/jit(take_along_axis)/gather | solution.py:31
  236.6 2.8 %copy.410 = f32[16,512,2]{1,0,2:T(8,128)S(1)} copy(f32[16,512,2]{2,1,0:T(8,128)} %bitcast.110) | data formatting | bytes 131072 | tf_op jit(solution)/shard_map/jit(take_along_axis)/gather | solution.py:31
  239.5 0.6 broadcast_multiply_fusion
  (31 shorter events, 0.5 us)
Async XLA Ops:
  6.5 13.8 %copy-start = (bf16[16,1920]{1,0:T(8,128)(2,1)S(1)}, bf16[16,1920]{1,0:T(8,128)(2,1)}, u32[]{:S(2)}) copy-start(bf16[16,1920]{1,0:T(8,128)(2,1)} %param.7) | copy-start | bytes 184324
  13.0 28.9 %all-to-all-start.1 = ((bf16[8,16,1]{0,2,1:T(2,128)(2,1)}), bf16[8,16,1]{0,2,1:T(2,128)(2,1)S(1)}, u32[]{:S(2)}, u32[]{:S(2)}) async-start(bf16[8,16,1]{0,2,1:T(2,128)(2,1)} %copy.395), calls=%async_computation.1 | async-start | bytes 16384 | tf_op jit(solution)/shard_map/all_to_all | solution.py:70
  21.1 15.8 %copy-start.1 = (s32[16]{0:T(128)S(1)}, s32[16]{0:T(128)}, u32[]{:S(2)}) copy-start(s32[16]{0:T(128)} %param.9) | copy-start | bytes 196
  21.2 27.2 %copy-start.4 = (s32[16,4]{0,1:T(4,128)S(1)}, s32[16,4]{0,1:T(4,128)}, u32[]{:S(2)}) copy-start(s32[16,4]{0,1:T(4,128)} %param.10) | copy-start | bytes 772
  27.5 41.3 %copy-start.2 = (f32[1,16,512]{2,1,0:T(8,128)S(1)}, f32[1,16,512]{2,1,0:T(8,128)}, u32[]{:S(2)}) copy-start(f32[1,16,512]{2,1,0:T(8,128)} %param.12) | copy-start | bytes 98308
  41.8 12.4 %all-to-all-start.2 = ((s32[8,16,1]{0,2,1:T(1,128)}), s32[8,16,1]{0,2,1:T(1,128)S(1)}, u32[]{:S(2)}, u32[]{:S(2)}) async-start(s32[8,16,1]{0,2,1:T(1,128)} %copy.398), calls=%async_computation.2 | async-start | bytes 16384 | tf_op jit(solution)/shard_map/all_to_all | solution.py:71
  54.2 10.9 %all-to-all-start = ((s32[8,16,1]{0,2,1:T(1,128)}), s32[8,16,1]{0,2,1:T(1,128)S(1)}, u32[]{:S(2)}, u32[]{:S(2)}) async-start(s32[8,16,1]{0,2,1:T(1,128)} %copy.392), calls=%async_computation | async-start | bytes 16384 | tf_op jit(solution)/shard_map/all_to_all | solution.py:72
  65.2 17.3 %all-to-all-start.3 = ((bf16[16,8,1,1920]{3,1,2,0:T(8,128)(2,1)}), bf16[16,8,1,1920]{3,1,2,0:T(8,128)(2,1)S(1)}, u32[]{:S(2)}, u32[]{:S(2)}) async-start(bf16[16,8,1,1920]{3,1,2,0:T(8,128)(2,1)} %constant_dynamic-update-slice_fusion), calls=%async_computation.3 | async-start | bytes 983040 | tf_op jit(solution)/shard_map/all_to_all | solution.py:65
  68.7 39.5 %all-reduce.4.cloned.1.call-start = ((), (), s32[]{:S(2)}) async-start(), calls=%async_computation.4 | async-start | bytes 245760 | tf_op jit(solution)/shard_map/psum | solution.py:84
  236.6 2.9 %copy-start.3 = (f32[1,16,512]{2,1,0:T(8,128)S(1)}, f32[1,16,512]{2,1,0:T(8,128)}, u32[]{:S(2)}) copy-start(f32[1,16,512]{2,1,0:T(8,128)} %param.13) | copy-start | bytes 98308
Sparse Core Ops, SparseCore 0:
  87.6 20.6 all-reduce.3
